TPU v7x, 32 devices: a whole 2x2x4 slice. The times are simulated.
32 devices in a mesh: blk: 8 (over z, x), head: 4 (over y, core).
Axes of the slice: x: 2, y: 2, z: 4, core: 2. Of those that a mesh axis runs over, the one named last changes fastest.
Arguments:
- hidden: bfloat16 [1024, 2048], P('blk', 'head'), may hold values from -6 to 6
- key_cache: bfloat16 [1024, 1024], P('blk', 'head'), may hold values from -6 to 6
- value_cache: bfloat16 [1024, 1024], P('blk', 'head'), may hold values from -6 to 6
- block_spans: int32 [3], replicated, may hold values from 1 to 4, 8 in all
- cached_counts: int32 [8], replicated, may hold values from 0 to 128, as said below
- expert_ids: int32 [1024, 4], P('blk'), may hold values from 0 to 63, all different within a row; in each aligned block of 128 rows (0 to 127, 128 to 255, ...) at most 10 rows name the same one
- gate_weights: float32 [1024, 4], P('blk'), may hold values from 0.06 to 0.6
- attention_gain: float32 [2048], replicated, may hold values from 0.1 to 1.9
- mixture_gain: float32 [2048], replicated, may hold values from 0.1 to 1.9
- query_gain: float32 [128], replicated, may hold values from 0.1 to 1.9
- key_gain: float32 [128], replicated, may hold values from 0.1 to 1.9
- query_weight: bfloat16 [2048, 1024], P(None, 'head'), may hold values from -0.125 to 0.125
- key_weight: bfloat16 [2048, 1024], P(None, 'head'), may hold values from -0.125 to 0.125
- value_weight: bfloat16 [2048, 1024], P(None, 'head'), may hold values from -0.125 to 0.125
- output_weight: bfloat16 [1024, 2048], P('head', 'blk'), may hold values from -0.5 to 0.5
- expert_gate: bfloat16 [128, 2048, 512], P('blk', None, 'head'), may hold values from -0.125 to 0.125
- expert_up: bfloat16 [128, 2048, 512], P('blk', None, 'head'), may hold values from -0.125 to 0.125
- expert_down: bfloat16 [128, 512, 2048], P('blk', 'head'), may hold values from -0.1875 to 0.1875
Outputs:
- attention_out: bfloat16 [1024, 2048], P('blk', 'head')
- layer_out: bfloat16 [1024, 2048], P('blk', 'head')
Inputs may be any that keep to these rules, and one draw needn't show every extreme that they name: `block_spans`: the requests occupy all 8 blocks together; some request occupies 4 blocks. `cached_counts`: live cache slots come first in a block; some block has all 128 live. `expert_ids`: A token's experts differ. In the rows of one block (128 tokens) no expert is named by more than 10 rows.
All inputs are finite; a program needn't handle non-finite values.
Results may differ from a plain program's by a relative error of at most 0.012.
Values may be sent and summed in bfloat16 or wider, within the bound.
A program may use at most 128 MiB of HBM per device.

v0:
```python
import jax
import jax.numpy as jnp
from jax import lax
from jax.sharding import PartitionSpec as P

HD = 128
EXPERTS = 64
TOPK = 4
HP = 2
SPAN = 4
CAP = 10


def passed_along(block, axis, distance):
    devices = range(lax.axis_size(axis))
    route = [(i - distance, i) for i in devices if i - distance in devices]
    return lax.ppermute(block, axis, route)


def row_norm(values, gain_vector):
    return (
        values * lax.rsqrt(jnp.mean(values * values, axis=-1, keepdims=True) + 1e-05) * gain_vector
    )


def head_norm(projected, gain_vector):
    shaped = projected.reshape(projected.shape[0], -1, HD)
    normed = row_norm(shaped, gain_vector)
    return normed.reshape(projected.shape).astype(jnp.bfloat16)


def block_requests(block_spans, block_count):
    boundary = jnp.cumsum(block_spans)
    blocks = jnp.arange(block_count, dtype=jnp.int32)
    return jnp.sum((blocks[:, None] >= boundary[None, :]).astype(jnp.int32), axis=1)


def attend(queries, key_rows, value_rows, allowed):
    head_count = queries.shape[1] // HD
    query_heads = queries.reshape(queries.shape[0], head_count, HD)
    key_heads = key_rows.reshape(key_rows.shape[0], head_count, HD)
    value_heads = value_rows.reshape(value_rows.shape[0], head_count, HD)
    scores = jnp.einsum(
        "qhd,khd->hqk", query_heads, key_heads, preferred_element_type=jnp.float32
    ) * HD ** (-0.5)
    weights = jnp.where(allowed[None, None, :], jnp.exp(scores), 0.0)
    denominator = jnp.sum(weights, axis=2)
    numerator = jnp.einsum(
        "hqk,khd->hqd",
        weights.astype(jnp.bfloat16),
        value_heads,
        preferred_element_type=jnp.float32,
    )
    context = numerator / denominator[:, :, None]
    return jnp.transpose(context, (1, 0, 2)).reshape(queries.shape[0], -1).astype(jnp.bfloat16)


def send_whole(token_rows, holder, block_count):
    outgoing = token_rows[holder].reshape(block_count, -1, token_rows.shape[1])
    return lax.all_to_all(outgoing, "blk", split_axis=0, concat_axis=0, tiled=True)


def local(
    hidden,
    key_cache,
    value_cache,
    block_spans,
    cached_counts,
    expert_ids,
    gate_weights,
    attention_gain,
    mixture_gain,
    query_gain,
    key_gain,
    query_weight,
    key_weight,
    value_weight,
    output_weight,
    expert_gate,
    expert_up,
    expert_down,
):
    full_rows = lax.all_gather(hidden, "head", axis=1, tiled=True)
    normed = row_norm(full_rows.astype(jnp.float32), attention_gain).astype(jnp.bfloat16)
    queries = head_norm(
        jnp.dot(normed, query_weight, preferred_element_type=jnp.float32), query_gain
    )
    new_keys = head_norm(jnp.dot(normed, key_weight, preferred_element_type=jnp.float32), key_gain)
    new_values = jnp.dot(normed, value_weight, preferred_element_type=jnp.float32).astype(
        jnp.bfloat16
    )
    old_keys = head_norm(key_cache.astype(jnp.float32), key_gain)
    key_value_pair = jnp.stack(
        [
            jnp.concatenate([old_keys, new_keys], axis=0),
            jnp.concatenate([value_cache, new_values], axis=0),
        ]
    )
    block_count = lax.axis_size("blk")
    block_index = lax.axis_index("blk")
    requests = block_requests(block_spans, block_count)
    cache_slots = key_cache.shape[0]
    new_slots = hidden.shape[0]

    def allowed_for(distance):
        source = block_index - distance
        inside = (source >= 0) & (source < block_count)
        clipped = jnp.clip(source, 0, block_count - 1)
        same_request = inside & (requests[clipped] == requests[block_index])
        live_slots = jnp.concatenate(
            [
                jnp.arange(cache_slots, dtype=jnp.int32) < cached_counts[clipped],
                jnp.ones((new_slots,), jnp.bool_),
            ]
        )
        return same_request & live_slots

    pair_list = [key_value_pair]
    mask_list = [allowed_for(0)]
    carried = key_value_pair
    for step_index in range(SPAN - 1):
        carried = passed_along(carried, "blk", 1)
        pair_list.append(carried)
        mask_list.append(allowed_for(step_index + 1))
    carried = key_value_pair
    for step_index in range(SPAN - 1):
        carried = passed_along(carried, "blk", -1)
        pair_list.append(carried)
        mask_list.append(allowed_for(-(step_index + 1)))
    all_pairs = jnp.concatenate(pair_list, axis=1)
    context = attend(queries, all_pairs[0], all_pairs[1], jnp.concatenate(mask_list))
    attention = jnp.dot(
        context,
        lax.all_gather(output_weight, "blk", axis=1, tiled=True),
        preferred_element_type=jnp.float32,
    )
    share_width = hidden.shape[1]
    share_start = lax.axis_index("head") * share_width
    hidden_share = hidden.astype(jnp.float32)
    attention_all = lax.psum(attention.astype(jnp.bfloat16), "head").astype(jnp.float32)
    after_full = full_rows.astype(jnp.float32) + attention_all
    mixed_in = row_norm(after_full, mixture_gain).astype(jnp.bfloat16)
    attention_share = lax.dynamic_slice_in_dim(attention_all, share_start, share_width, 1)
    after_share = hidden_share + attention_share
    token_count = hidden.shape[0]
    flat_ids = expert_ids.reshape(-1)
    onehot = (flat_ids[:, None] == jnp.arange(EXPERTS, dtype=jnp.int32)[None, :]).astype(jnp.int32)
    rank_table = jnp.cumsum(onehot, axis=0) - onehot
    position = jnp.sum(rank_table * onehot, axis=1).reshape(token_count, TOPK)
    slot_index = (
        expert_ids[:, :, None] * HP + jnp.arange(HP, dtype=jnp.int32)[None, None, :]
    ) * CAP + position[:, :, None]
    token_numbers = jnp.broadcast_to(
        jnp.arange(token_count, dtype=jnp.int32)[:, None, None], slot_index.shape
    )
    holder = (
        jnp.full((EXPERTS * HP * CAP,), token_count, jnp.int32)
        .at[slot_index.reshape(-1)]
        .set(token_numbers.reshape(-1))
    )
    token_rows = jnp.concatenate(
        [mixed_in, jnp.zeros((1, mixed_in.shape[1]), jnp.bfloat16)], axis=0
    )
    slots_here = expert_gate.shape[0]
    incoming = send_whole(token_rows, holder, block_count)
    grouped = incoming.reshape(block_count, slots_here, CAP, incoming.shape[2])
    gate_part = jnp.einsum(
        "nlcd,ldf->nlcf", grouped, expert_gate, preferred_element_type=jnp.float32
    )
    up_part = jnp.einsum("nlcd,ldf->nlcf", grouped, expert_up, preferred_element_type=jnp.float32)
    activation = (jax.nn.silu(gate_part) * up_part).astype(jnp.bfloat16)
    produced = jnp.einsum(
        "nlcf,lfd->nlcd", activation, expert_down, preferred_element_type=jnp.float32
    ).astype(jnp.bfloat16)
    returned = lax.all_to_all(
        produced.reshape(block_count, slots_here * CAP, produced.shape[3]),
        "blk",
        split_axis=0,
        concat_axis=0,
        tiled=True,
    )
    flat_returned = returned.reshape(-1, returned.shape[2])
    picked = flat_returned[slot_index.reshape(token_count, TOPK * HP)]
    weights = jnp.repeat(gate_weights, HP, axis=1)
    mixture_partial = jnp.sum(picked.astype(jnp.float32) * weights[:, :, None], axis=1)
    mixture_share = lax.psum_scatter(
        mixture_partial.astype(jnp.bfloat16), "head", scatter_dimension=1, tiled=True
    ).astype(jnp.float32)
    attention_out = attention_share.astype(jnp.bfloat16)
    layer_out = (after_share + mixture_share).astype(jnp.bfloat16)
    return (attention_out, layer_out)


def solution(mesh):
    placed = (
        P("blk", "head"),
        P("blk", "head"),
        P("blk", "head"),
        P(),
        P(),
        P("blk", None),
        P("blk", None),
        P(),
        P(),
        P(),
        P(),
        P(None, "head"),
        P(None, "head"),
        P(None, "head"),
        P("head", "blk"),
        P("blk", None, "head"),
        P("blk", None, "head"),
        P("blk", "head", None),
    )
    return jax.shard_map(
        local,
        mesh=mesh,
        in_specs=placed,
        out_specs=(P("blk", "head"), P("blk", "head")),
        check_vma=False,
    )
```

profile of v0, /device:TPU:10, one launch (start us, length us, event | category | flops | bytes accessed | tf_op | source)
XLA Modules:
  0.0 437.7 jit_solution(6130366800271686828)
XLA Ops:
  7.3 7.5 %all_gather.6 = bf16[128,2048]{1,0:T(8,128)(2,1)S(1)} all-gather(bf16[128,512]{1,0:T(8,128)(2,1)} %param.18), channel_id=1, replica_groups=mesh['blk'=8,'head'=4] {'head'}, dimensions={1}, use_global_device_ids=true | all-gather | bytes 655360 | tf_op jit(solution)/shard_map/all_gather | solution.py:83
  15.1 1.0 fusion.54
  16.4 0.9 convert_multiply_fusion.4
  17.6 0.7 broadcast_bitcast_fusion
  18.3 1.6 convolution_convert_fusion.1
  20.4 0.7 pad_maximum_fusion
  21.1 3.4 collective-permute-start
  24.6 2.4 collective-permute-start.3
  27.7 0.7 fusion.52
  28.4 0.6 iota_compare_fusion.9
  29.1 0.6 iota_compare_fusion.8
  29.7 0.6 iota_compare_fusion.7
  30.3 0.7 iota_compare_fusion.6
  31.0 0.6 iota_compare_fusion.5
  31.5 0.6 iota_compare_fusion.4
  32.2 0.7 iota_compare_fusion.3
  32.9 0.4 fusion.55
  33.6 1.2 reduce-window.19
  34.8 0.2 slice_reduce_fusion
  35.6 0.3 add.211
  40.6 4.4 collective-permute-start.1
  47.4 1.9 collective-permute-start.4
  50.5 0.6 collective-permute-done.1
  51.2 5.3 %collective-permute-start.2 = (bf16[2,256,256]{2,1,0:T(8,128)(2,1)S(1)}, bf16[2,256,256]{2,1,0:T(8,128)(2,1)S(1)}, u32[]{:S(2)}, u32[]{:S(2)}) collective-permute-start(bf16[2,256,256]{2,1,0:T(8,128)(2,1)S(1)} %collective-permute-done.1), channel_id=1, source_target_pairs={{0,4},{4,8},{8,12},{12,16},{16,20},{20,24},{24,28},{1,5},{5,9},{9,... | collective-permute-start | bytes 786440 | tf_op jit(solution)/shard_map/ppermute | solution.py:17
  56.6 0.2 reshape.277
  56.8 0.2 dynamic-update-slice.7
  57.1 0.2 dynamic-update-slice.8
  57.3 0.2 dynamic-update-slice.9
  57.5 0.2 dynamic-update-slice.10
  58.3 4.3 scatter_custom_fusion
  62.6 0.7 constant_dynamic-update-slice_fusion.5
  63.3 0.5 collective-permute-done.4
  63.9 5.0 %collective-permute-start.5 = (bf16[2,256,256]{2,1,0:T(8,128)(2,1)S(1)}, bf16[2,256,256]{2,1,0:T(8,128)(2,1)S(1)}, u32[]{:S(2)}, u32[]{:S(2)}) collective-permute-start(bf16[2,256,256]{2,1,0:T(8,128)(2,1)S(1)} %collective-permute-done.4), channel_id=1, source_target_pairs={{4,0},{8,4},{12,8},{16,12},{20,16},{24,20},{28,24},{5,1},{9,5},{13... | collective-permute-start | bytes 786440 | tf_op jit(solution)/shard_map/ppermute | solution.py:17
  68.8 0.7 constant_dynamic-update-slice_fusion.4
  69.6 5.2 %collective-permute-done.2 = bf16[2,256,256]{2,1,0:T(8,128)(2,1)S(1)} collective-permute-done((bf16[2,256,256]{2,1,0:T(8,128)(2,1)S(1)}, bf16[2,256,256]{2,1,0:T(8,128)(2,1)S(1)}, u32[]{:S(2)}, u32[]{:S(2)}) %collective-permute-start.2) | collective-permute-done | bytes 262176 | tf_op jit(solution)/shard_map/ppermute | solution.py:17
  74.7 0.7 constant_dynamic-update-slice_fusion.3
  75.4 0.7 constant_dynamic-update-slice_fusion.2
  76.2 0.7 constant_dynamic-update-slice_fusion.1
  76.9 0.7 constant_dynamic-update-slice_fusion
  77.6 1.6 fusion.51
  79.2 0.2 reshape_squeeze.6
  79.4 0.6 copy.107
  80.2 0.7 fusion.56
  80.9 0.4 fusion.24
  81.3 2.3 convolution_convert_fusion
  83.7 33.0 %all-reduce.10.cloned.1.call-done = bf16[128,2048]{1,0:T(8,128)(2,1)} async-done(((bf16[128,2048]{1,0:T(8,128)(2,1)}), bf16[128,2048]{1,0:T(8,128)(2,1)}) %all-reduce.10.cloned.1.call-update) | async-done | bytes 524304 | tf_op jit(solution)/shard_map/psum | solution.py:140
  116.8 1.3 multiply_reduce_fusion
  118.1 1.3 multiply_convert_fusion
  119.4 6.1 %gather_fusion = bf16[1280,2048]{1,0:T(8,128)(2,1)} fusion(bf16[129,2048]{1,0:T(8,128)(2,1)S(1)} %concatenate.47, s32[2048]{0:T(1024)S(1)} %pad_clamp_fusion), kind=kCustom, calls=%fused_computation | custom fusion | bytes 10490880 | tf_op jit(solution)/shard_map/gather | solution.py:59
  125.5 119.0 %all_to_all.10 = bf16[8,160,2048]{2,1,0:T(8,128)(2,1)} all-to-all(bf16[8,160,2048]{2,1,0:T(8,128)(2,1)} %bitcast.145), channel_id=1, replica_groups=mesh['blk'=8,'head'=4] {'blk'}, dimensions={0} | all-to-all | bytes 10485760 | tf_op jit(solution)/shard_map/all_to_all | solution.py:60
  244.5 5.5 %copy.98 = bf16[8,160,2048]{2,0,1:T(8,128)(2,1)S(1)} copy(bf16[8,160,2048]{2,1,0:T(8,128)(2,1)} %all_to_all.10) | data formatting | bytes 10485760 | tf_op jit(solution)/shard_map/all_to_all | solution.py:60
  250.0 1.5 fusion.11
  251.6 0.7 slice-done.3
  252.2 1.5 fusion.20
  253.7 5.7 %convert_bitcast_fusion = bf16[8,16,10,2048]{3,2,0,1:T(8,128)(2,1)S(1)} fusion(bf16[16,128,2048]{2,1,0:T(8,128)(2,1)} %param.35, bf16[8,16,10,128]{3,0,2,1:T(8,128)(2,1)S(1)} %fusion.20), kind=kOutput, calls=%fused_computation.11 | convolution fusion | flops 673710080 | bytes 13959168 | tf_op jit(solution)/shard_map/nlcf,lfd->nlcd/dot_general | solution.py:172
  259.5 4.1 copy.100
  263.6 5.2 %copy.101 = bf16[8,160,2048]{2,1,0:T(8,128)(2,1)} copy(bf16[8,160,2048]{2,0,1:T(8,128)(2,1)S(1)} %bitcast.146) | data formatting | bytes 10485760 | tf_op jit(solution)/shard_map/reshape | solution.py:176
  268.8 7.1 %all-to-all-start.1 = ((bf16[8,160,2048]{2,1,0:T(8,128)(2,1)}), bf16[8,160,2048]{2,1,0:T(8,128)(2,1)}, u32[]{:S(2)}, u32[]{:S(2)}) async-start(bf16[8,160,2048]{2,1,0:T(8,128)(2,1)} %copy.101), calls=%async_computation.1 | async-start | bytes 10485760 | tf_op jit(solution)/shard_map/all_to_all | solution.py:175
  276.4 110.8 %all-to-all-done.1 = bf16[8,160,2048]{2,1,0:T(8,128)(2,1)} async-done(((bf16[8,160,2048]{2,1,0:T(8,128)(2,1)}), bf16[8,160,2048]{2,1,0:T(8,128)(2,1)}, u32[]{:S(2)}, u32[]{:S(2)}) %all-to-all-start.1) | async-done | bytes 5242912 | tf_op jit(solution)/shard_map/all_to_all | solution.py:175
  387.2 12.1 %gather_fusion.1 = bf16[1024,2048]{1,0:T(8,128)(2,1)} fusion(bf16[1280,2048]{1,0:T(8,128)(2,1)} %bitcast.38, s32[1024]{0:T(1024)S(1)} %broadcast_clamp_fusion), kind=kCustom, calls=%fused_computation.1 | custom fusion | bytes 8392704 | tf_op jit(solution)/shard_map/gather | solution.py:183
  399.4 7.4 %fusion = bf16[128,2048]{1,0:T(8,128)(2,1)} fusion(bf16[1024,2048]{1,0:T(8,128)(2,1)} %gather_fusion.1, f32[128,8]{1,0:T(8,128)S(1)} %copy.103), kind=kLoop, calls=%fused_computation.4 | loop fusion | flops 6029312 | bytes 4722688 | tf_op jit(solution)/shard_map/reduce_sum | solution.py:185
  406.9 0.7 dynamic-slice_convert_fusion
  407.6 22.0 %reduce-scatter.2.cloned.1.call-done = bf16[128,512]{1,0:T(8,128)(2,1)} async-done(((bf16[128,2048]{1,0:T(8,128)(2,1)}), bf16[128,512]{1,0:T(8,128)(2,1)}) %reduce-scatter.2.cloned.1.call-update) | async-done | bytes 131088 | tf_op jit(solution)/shard_map/reduce_scatter | solution.py:186
  429.6 1.6 add_convert_fusion
  (106 shorter events, 4.4 us)
Async XLA Ops:
  7.2 7.9 %copy-start = (bf16[2048,256]{1,0:T(8,128)(2,1)S(1)}, bf16[2048,256]{1,0:T(8,128)(2,1)}, u32[]{:S(2)}) copy-start(bf16[2048,256]{1,0:T(8,128)(2,1)} %param.30) | copy-start | bytes 3145732
  7.2 25.7 %copy-start.11 = (f32[2048]{0:T(1024)S(1)}, f32[2048]{0:T(1024)}, u32[]{:S(2)}) copy-start(f32[2048]{0:T(1024)} %param.25) | copy-start | bytes 24580
  7.2 13.1 %copy-start.4 = (bf16[128,256]{1,0:T(8,128)(2,1)S(1)}, bf16[128,256]{1,0:T(8,128)(2,1)}, u32[]{:S(2)}) copy-start(bf16[128,256]{1,0:T(8,128)(2,1)} %param.19) | copy-start | bytes 196612
  7.2 13.1 %copy-start.5 = (bf16[128,256]{1,0:T(8,128)(2,1)S(1)}, bf16[128,256]{1,0:T(8,128)(2,1)}, u32[]{:S(2)}) copy-start(bf16[128,256]{1,0:T(8,128)(2,1)} %param.20) | copy-start | bytes 196612
  7.2 19.8 %copy-start.8 = (s32[128,4]{0,1:T(4,128)S(1)}, s32[128,4]{0,1:T(4,128)}, u32[]{:S(2)}) copy-start(s32[128,4]{0,1:T(4,128)} %param.23) | copy-start | bytes 6148
  7.2 20.2 %copy-start.12 = (s32[3]{0:T(128)S(1)}, s32[3]{0:T(128)}, u32[]{:S(2)}) copy-start(s32[3]{0:T(128)} %param.21) | copy-start | bytes 40
  7.2 20.4 %copy-start.6 = (s32[8]{0:T(128)S(1)}, s32[8]{0:T(128)}, u32[]{:S(2)}) copy-start(s32[8]{0:T(128)} %param.22) | copy-start | bytes 100
  7.2 25.6 %copy-start.10 = (bf16[2048,256]{1,0:T(8,128)(2,1)S(1)}, bf16[2048,256]{1,0:T(8,128)(2,1)}, u32[]{:S(2)}) copy-start(bf16[2048,256]{1,0:T(8,128)(2,1)} %param.29) | copy-start | bytes 3145732
  7.3 74.1 %all-gather.2.cloned.1.call-start = ((), (), s32[]{:S(2)}) async-start(), calls=%async_computation.3 | async-start | bytes 1179648 | tf_op jit(solution)/shard_map/all_gather | solution.py:134
  15.0 18.5 %copy-start.13 = (f32[128]{0:T(128)S(1)}, f32[128]{0:T(128)}, u32[]{:S(2)}) copy-start(f32[128]{0:T(128)} %param.27) | copy-start | bytes 1540
  21.1 19.5 %collective-permute-start = (bf16[2,256,256]{2,1,0:T(8,128)(2,1)S(1)}, bf16[2,256,256]{2,1,0:T(8,128)(2,1)S(1)}, u32[]{:S(2)}, u32[]{:S(2)}) collective-permute-start(bf16[2,256,256]{2,1,0:T(8,128)(2,1)S(1)} %get-tuple-element.4), channel_id=1, source_target_pairs={{0,4},{4,8},{8,12},{12,16},{16,20},{20,24},{24,28},{1,5},{5,9},{9,... | collective-permute-start | bytes 786440 | tf_op jit(solution)/shard_map/ppermute | solution.py:17
  24.6 22.8 %collective-permute-start.3 = (bf16[2,256,256]{2,1,0:T(8,128)(2,1)S(1)}, bf16[2,256,256]{2,1,0:T(8,128)(2,1)S(1)}, u32[]{:S(2)}, u32[]{:S(2)}) collective-permute-start(bf16[2,256,256]{2,1,0:T(8,128)(2,1)S(1)} %get-tuple-element.4), channel_id=1, source_target_pairs={{4,0},{8,4},{12,8},{16,12},{20,16},{24,20},{28,24},{5,1},{9,5},{13... | collective-permute-start | bytes 786440 | tf_op jit(solution)/shard_map/ppermute | solution.py:17
  27.0 89.8 %all-reduce.10.cloned.1.call-start = ((), (), s32[]{:S(2)}) async-start(), calls=%async_computation.4 | async-start | bytes 1048576 | tf_op jit(solution)/shard_map/psum | solution.py:140
  40.6 10.6 %collective-permute-start.1 = (bf16[2,256,256]{2,1,0:T(8,128)(2,1)S(1)}, bf16[2,256,256]{2,1,0:T(8,128)(2,1)S(1)}, u32[]{:S(2)}, u32[]{:S(2)}) collective-permute-start(bf16[2,256,256]{2,1,0:T(8,128)(2,1)S(1)} %collective-permute-done), channel_id=1, source_target_pairs={{0,4},{4,8},{8,12},{12,16},{16,20},{20,24},{24,28},{1,5},{5,9},{9,... | collective-permute-start | bytes 786440 | tf_op jit(solution)/shard_map/ppermute | solution.py:17
  47.4 16.5 %collective-permute-start.4 = (bf16[2,256,256]{2,1,0:T(8,128)(2,1)S(1)}, bf16[2,256,256]{2,1,0:T(8,128)(2,1)S(1)}, u32[]{:S(2)}, u32[]{:S(2)}) collective-permute-start(bf16[2,256,256]{2,1,0:T(8,128)(2,1)S(1)} %collective-permute-done.3), channel_id=1, source_target_pairs={{4,0},{8,4},{12,8},{16,12},{20,16},{24,20},{28,24},{5,1},{9,5},{13... | collective-permute-start | bytes 786440 | tf_op jit(solution)/shard_map/ppermute | solution.py:17
  51.2 23.6 %collective-permute-start.2 = (bf16[2,256,256]{2,1,0:T(8,128)(2,1)S(1)}, bf16[2,256,256]{2,1,0:T(8,128)(2,1)S(1)}, u32[]{:S(2)}, u32[]{:S(2)}) collective-permute-start(bf16[2,256,256]{2,1,0:T(8,128)(2,1)S(1)} %collective-permute-done.1), channel_id=1, source_target_pairs={{0,4},{4,8},{8,12},{12,16},{16,20},{20,24},{24,28},{1,5},{5,9},{9,... | collective-permute-start | bytes 786440 | tf_op jit(solution)/shard_map/ppermute | solution.py:17
  63.9 13.0 %collective-permute-start.5 = (bf16[2,256,256]{2,1,0:T(8,128)(2,1)S(1)}, bf16[2,256,256]{2,1,0:T(8,128)(2,1)S(1)}, u32[]{:S(2)}, u32[]{:S(2)}) collective-permute-start(bf16[2,256,256]{2,1,0:T(8,128)(2,1)S(1)} %collective-permute-done.4), channel_id=1, source_target_pairs={{4,0},{8,4},{12,8},{16,12},{20,16},{24,20},{28,24},{5,1},{9,5},{13... | collective-permute-start | bytes 786440 | tf_op jit(solution)/shard_map/ppermute | solution.py:17
  79.4 38.6 %copy-start.7 = (f32[2048]{0:T(1024)S(1)}, f32[2048]{0:T(1024)}, u32[]{:S(2)}) copy-start(f32[2048]{0:T(1024)} %param.26) | copy-start | bytes 24580
  125.5 124.5 %slice-start = ((s8[8388608]{0:T(1024)(128)(4,1)}), s8[4194304]{0:T(1024)(128)(4,1)S(1)}, s32[]{:S(2)}) async-start(s8[8388608]{0:T(1024)(128)(4,1)} %bitcast.141), calls=%async_computation.6 | async-start | bytes 8388608
  244.5 5.5 %slice-start.1 = ((s8[8388608]{0:T(1024)(128)(4,1)}), s8[4194304]{0:T(1024)(128)(4,1)S(1)}, s32[]{:S(2)}) async-start(s8[8388608]{0:T(1024)(128)(4,1)} %bitcast.141), calls=%async_computation.7 | async-start | bytes 8388608
  244.5 7.1 %slice-start.2 = ((s8[8388608]{0:T(1024)(128)(4,1)}), s8[4194304]{0:T(1024)(128)(4,1)S(1)}, s32[]{:S(2)}) async-start(s8[8388608]{0:T(1024)(128)(4,1)} %bitcast.143), calls=%async_computation.8 | async-start | bytes 8388608
  250.0 2.2 slice-start.3
  268.8 7.5 %copy-start.9 = (f32[128,4]{0,1:T(4,128)S(1)}, f32[128,4]{0,1:T(4,128)}, u32[]{:S(2)}) copy-start(f32[128,4]{0,1:T(4,128)} %param.24) | copy-start | bytes 6148
  268.8 118.4 %all-to-all-start.1 = ((bf16[8,160,2048]{2,1,0:T(8,128)(2,1)}), bf16[8,160,2048]{2,1,0:T(8,128)(2,1)}, u32[]{:S(2)}, u32[]{:S(2)}) async-start(bf16[8,160,2048]{2,1,0:T(8,128)(2,1)} %copy.101), calls=%async_computation.1 | async-start | bytes 10485760 | tf_op jit(solution)/shard_map/all_to_all | solution.py:175
  275.9 153.7 %reduce-scatter.2.cloned.1.call-start = ((), (), s32[]{:S(2)}) async-start(), calls=%async_computation.5 | async-start | bytes 655360 | tf_op jit(solution)/shard_map/reduce_scatter | solution.py:186
  387.2 44.0 %copy-start.1 = (bf16[2048,256]{1,0:T(8,128)(2,1)S(1)}, bf16[2048,256]{1,0:T(8,128)(2,1)}, u32[]{:S(2)}) copy-start(bf16[2048,256]{1,0:T(8,128)(2,1)} %param.30) | copy-start | bytes 3145732
  399.4 7.4 %copy-start.2 = (bf16[128,2048]{1,0:T(8,128)(2,1)S(1)}, bf16[128,2048]{1,0:T(8,128)(2,1)}, u32[]{:S(2)}) copy-start(bf16[128,2048]{1,0:T(8,128)(2,1)} %all-reduce.10.cloned.1.call-done) | copy-start | bytes 1572868
  399.4 30.2 %copy-start.3 = (bf16[128,512]{1,0:T(8,128)(2,1)S(1)}, bf16[128,512]{1,0:T(8,128)(2,1)}, u32[]{:S(2)}) copy-start(bf16[128,512]{1,0:T(8,128)(2,1)} %param.18) | copy-start | bytes 393220
Sparse Core Ops, SparseCore 0:
  27.1 51.2 all-gather.1
  83.8 32.8 all-reduce.9
  406.9 22.6 reduce-scatter.1
where the time goes:
time: 440 us; the launch traced here: 438 us
  waiting for transfers between devices  172 us (39%)
  blocking collectives  127 us (29%)
  local copies, waits for them, and re-layouts  51.1 us (12%)
  starting transfers between devices  29.6 us (7%)
  between operations  22.7 us (5%)
  other arithmetic  20.4 us (5%)
  matrix products  15.2 us (3%)
    all_to_all x1, blocking collectives, send_whole(): lax.all_to_all(outgoing, 'blk', split_axis=0, concat_axis=0, tiled=True)  119 us
    all_to_all x1, waiting for transfers between devices, local(): lax.all_to_all(produced.reshape(block_count, slots_here * CAP, produced.s...  111 us
    psum x1, waiting for transfers between devices, local(): lax.psum(attention.astype(jnp.bfloat16), 'head').astype(jnp.float32)  33 us
    ppermute x6, starting transfers between devices, passed_along(): return lax.ppermute(block, axis, route)  22.4 us
    reduce_scatter x1, waiting for transfers between devices, local(): lax.psum_scatter(mixture_partial.astype(jnp.bfloat16), 'head', scatter_di...  22 us
    gather x1, local copies, waits for them, and re-layouts, local(): picked = flat_returned[slot_index.reshape(token_count, TOPK * HP)]  12.1 us
  transfers between devices with their start and end apart: 10, of which 6 were waited for; matrix products, arithmetic and copies ran while one was open for 5% of the time, Pallas kernels for 0%

commit v1 on v0

v1 whole, which is shorter than its diff:
```python
import functools

import jax
import jax.numpy as jnp
from jax import lax
from jax.experimental import pallas as pl
from jax.experimental.pallas import tpu as pltpu
from jax.sharding import PartitionSpec as P

HD = 128
EXPERTS = 64
TOPK = 4
HP = 2
SPAN = 4
CAP = 10
REACH = SPAN - 1
LANES = 128
F32 = jnp.float32
BF16 = jnp.bfloat16
MESH = pl.DeviceIdType.MESH
DISTANCES = (1, -1, 2, -2, 3, -3)


def dot(left, right):
    return jnp.dot(left, right, preferred_element_type=F32)


def head_norm(projected, gain):
    parts = []
    for first in range(0, projected.shape[1], HD):
        head = projected[:, first : first + HD]
        scale = lax.rsqrt(jnp.mean(head * head, axis=-1, keepdims=True) + 1e-05)
        parts.append((head * scale * gain).astype(BF16))
    return jnp.concatenate(parts, axis=1)


def attention_kernel(
    blocks, heads,
    hidden, key_cache, value_cache, attention_gain, query_gain, key_gain, mask,
    query_weight, key_weight, value_weight,
    context,
    rows, pairs, numerator, denominator,
    row_send, row_recv, pair_send, pair_recv,
):
    blk, head = lax.axis_index("blk"), lax.axis_index("head")
    inside = lambda block: (block >= 0) & (block < blocks)

    barrier = pltpu.get_barrier_semaphore()
    for step in range(1, heads):
        pl.semaphore_signal(
            barrier, inc=1, device_id=(blk, lax.rem(head + step, heads)), device_id_type=MESH
        )
    for distance in DISTANCES:
        @pl.when(inside(blk + distance))
        def _():
            pl.semaphore_signal(
                barrier, inc=1, device_id=(blk + distance, head), device_id_type=MESH
            )
    near = sum(jnp.where(inside(blk + distance), 1, 0) for distance in DISTANCES)
    pl.semaphore_wait(barrier, heads - 1 + near)

    def row_copy(step):
        return pltpu.make_async_remote_copy(
            src_ref=hidden, dst_ref=rows.at[head],
            send_sem=row_send.at[step], recv_sem=row_recv.at[head],
            device_id=(blk, lax.rem(head + step, heads)), device_id_type=MESH,
        )

    def row_arrival(source):
        return pltpu.make_async_remote_copy(
            src_ref=hidden, dst_ref=rows.at[source],
            send_sem=row_send.at[0], recv_sem=row_recv.at[source],
            device_id=(blk, source), device_id_type=MESH,
        )

    def pair_copy(distance, part):
        slot = distance + REACH
        return pltpu.make_async_remote_copy(
            src_ref=pairs.at[REACH, pl.ds(2 * part, 2)],
            dst_ref=pairs.at[slot, pl.ds(2 * part, 2)],
            send_sem=pair_send.at[slot, part], recv_sem=pair_recv.at[slot, part],
            device_id=(blk + distance, head), device_id_type=MESH,
        )

    for step in range(1, heads):
        row_copy(step).start()
    rows[head] = hidden[...]

    def send_pairs(part):
        for distance in DISTANCES:
            @pl.when(inside(blk + distance))
            def _():
                pair_copy(distance, part).start()

    pairs[REACH, 0] = head_norm(key_cache[...].astype(F32), key_gain[...])
    pairs[REACH, 1] = value_cache[...]
    send_pairs(0)

    for step in range(1, heads):
        row_arrival(lax.rem(head + step, heads)).wait_recv()
    width = hidden.shape[1]
    square = jnp.zeros((hidden.shape[0], 1), F32)
    for source in range(heads):
        piece = rows[source].astype(F32)
        square += jnp.sum(piece * piece, axis=-1, keepdims=True)
    scale = lax.rsqrt(square / (heads * width) + 1e-05)
    normed = jnp.concatenate(
        [
            (rows[source].astype(F32) * scale * attention_gain[:, source * width : (source + 1) * width]).astype(BF16)
            for source in range(heads)
        ],
        axis=1,
    )
    pairs[REACH, 2] = head_norm(dot(normed, key_weight[...]), key_gain[...])
    pairs[REACH, 3] = dot(normed, value_weight[...]).astype(BF16)
    send_pairs(1)
    queries = head_norm(dot(normed, query_weight[...]), query_gain[...])

    numerator[...] = jnp.zeros_like(numerator)
    denominator[...] = jnp.zeros_like(denominator)
    head_count = queries.shape[1] // HD

    def attend(slot, part):
        allowed = mask[slot, part] > 0.0
        for index in range(head_count):
            lanes = slice(index * HD, (index + 1) * HD)
            keys = pairs[slot, 2 * part][:, lanes]
            values = pairs[slot, 2 * part + 1][:, lanes]
            scores = lax.dot_general(
                queries[:, lanes], keys, (((1,), (1,)), ((), ())), preferred_element_type=F32
            ) * HD ** (-0.5)
            weights = jnp.where(allowed, jnp.exp(scores), 0.0)
            denominator[index] += jnp.sum(weights, axis=1, keepdims=True)
            numerator[index] += dot(weights.astype(BF16), values)

    attend(REACH, 0)
    attend(REACH, 1)
    for part in range(2):
        for distance in DISTANCES:
            @pl.when(inside(blk - distance))
            def _():
                pair_copy(distance, part).wait_recv()
                attend(distance + REACH, part)
    context[...] = jnp.concatenate(
        [numerator[index] / denominator[index] for index in range(head_count)], axis=1
    ).astype(BF16)
    for step in range(1, heads):
        row_copy(step).wait_send()
    for part in range(2):
        for distance in DISTANCES:
            @pl.when(inside(blk + distance))
            def _():
                pair_copy(distance, part).wait_send()


def mixture_kernel(
    blocks, heads, stride, merged,
    context, output_weight, hidden, dispatch, combine, mixture_gain,
    expert_gate, expert_up, expert_down,
    attention_out, layer_out,
    partial, arrived, after,
    outgoing, gathered, slabs, gates, ups, downs,
    pair_out, pair_in, cross_out, cross_in, back_out, back_in,
    share_send, share_recv, weight_sem,
    all_send, all_recv, core_send, core_recv, side_send, side_recv, relay_send, relay_recv,
    pair_send, pair_recv, cross_send, cross_recv, back_send, back_recv,
):
    blk, head = lax.axis_index("blk"), lax.axis_index("head")
    core_peer = head + 1 - 2 * lax.rem(head, 2)
    side_peer = lax.rem(head + 2, 4)
    far_peer = lax.rem(core_peer + 2, 4)
    room = outgoing.shape[1]
    width = hidden.shape[1]
    share = width // LANES
    groups = expert_gate.shape[0] // merged

    def remote(source, target, send, recv, where):
        return pltpu.make_async_remote_copy(
            src_ref=source, dst_ref=target, send_sem=send, recv_sem=recv,
            device_id=where, device_id_type=MESH,
        )

    def weight_copies(index):
        units = pl.ds(index * merged, merged)
        return [
            pltpu.make_async_copy(source.at[units], target.at[units], weight_sem.at[kind, index])
            for kind, (source, target) in enumerate(
                ((expert_gate, gates), (expert_up, ups), (expert_down, downs))
            )
        ]

    @pl.loop(0, groups)
    def _(index):
        for copy in weight_copies(index):
            copy.start()

    barrier = pltpu.get_barrier_semaphore()
    for step in range(1, heads):
        pl.semaphore_signal(
            barrier, inc=1, device_id=(blk, lax.rem(head + step, heads)), device_id_type=MESH
        )

    @pl.loop(1, blocks)
    def _(step):
        pl.semaphore_signal(
            barrier, inc=1, device_id=(lax.rem(blk + step, blocks), head), device_id_type=MESH
        )

    def share_copy(step):
        target = lax.rem(head + step, heads)
        return remote(
            partial.at[target], arrived.at[step], share_send.at[step], share_recv.at[step],
            (blk, target),
        )

    ctx = context[...]
    for index in range(heads):
        partial[index] = dot(ctx, output_weight[:, index * width : (index + 1) * width]).astype(BF16)
    pl.semaphore_wait(barrier, heads - 1 + blocks - 1)
    for step in range(1, heads):
        share_copy(step).start()
    total = partial[head].astype(F32)
    for step in range(1, heads):
        share_copy(step).wait_recv()
        total = total + arrived[step].astype(F32)
    attention_out[...] = total.astype(BF16)
    total = total + hidden[...].astype(F32)
    after[...] = total
    rounded = total.astype(BF16)

    def all_copy(step):
        target = lax.rem(blk + step, blocks)
        return remote(
            outgoing.at[target], gathered.at[head, blk], all_send.at[step], all_recv.at[step],
            (target, head),
        )

    def all_arrival(step):
        source = lax.rem(blk - step + blocks, blocks)
        return remote(
            outgoing.at[source], gathered.at[head, source], all_send.at[step], all_recv.at[step],
            (source, head),
        )

    def core_copy(source, step):
        return remote(
            gathered.at[head, source], gathered.at[head, source],
            core_send.at[step], core_recv.at[step], (blk, core_peer),
        )

    def side_copy(source, step):
        return remote(
            gathered.at[head, source], gathered.at[head, source],
            side_send.at[step], side_recv.at[step], (blk, side_peer),
        )

    def relay_copy(source, step):
        return remote(
            gathered.at[side_peer, source], gathered.at[side_peer, source],
            relay_send.at[step], relay_recv.at[step], (blk, core_peer),
        )

    def arrival(owner, source, send, recv):
        return remote(
            gathered.at[owner, source], gathered.at[owner, source], send, recv, (blk, core_peer)
        )

    @pl.loop(1, blocks)
    def _(step):
        target = lax.rem(blk + step, blocks)
        outgoing[target] = dot(dispatch[target], rounded).astype(BF16)
        all_copy(step).start()

    gathered[head, blk] = dot(dispatch[blk], rounded).astype(BF16)
    core_copy(blk, 0).start()
    side_copy(blk, 0).start()

    @pl.loop(1, blocks)
    def _(step):
        source = lax.rem(blk - step + blocks, blocks)
        all_arrival(step).wait_recv()
        core_copy(source, step).start()
        side_copy(source, step).start()

    @pl.loop(0, blocks)
    def _(step):
        source = lax.rem(blk - step + blocks, blocks)
        arrival(side_peer, source, side_send.at[step], side_recv.at[step]).wait_recv()
        relay_copy(source, step).start()

    @pl.loop(0, blocks)
    def _(step):
        source = lax.rem(blk - step + blocks, blocks)
        arrival(core_peer, source, core_send.at[step], core_recv.at[step]).wait_recv()
        arrival(far_peer, source, relay_send.at[step], relay_recv.at[step]).wait_recv()
        square = jnp.zeros((room, 1), F32)
        for index in range(heads):
            piece = gathered[index, source].astype(F32)
            square += jnp.sum(piece * piece, axis=-1, keepdims=True)
        scale = lax.rsqrt(square / (heads * width) + 1e-05)
        place = pl.ds(pl.multiple_of(source * room, 16), room)
        for index in range(heads):
            normed = gathered[index, source].astype(F32) * scale
            for lane in range(share):
                slab = index * share + lane
                slabs[slab, place, :] = (
                    normed[:, lane * LANES : (lane + 1) * LANES]
                    * mixture_gain[:, slab * LANES : (slab + 1) * LANES]
                )

    depth = heads * share

    @pl.loop(0, groups)
    def _(index):
        for copy in weight_copies(index):
            copy.wait()
        mine = pl.ds(index, blocks * room // stride, stride) if stride > 1 else pl.ds(0, blocks * room)
        tokens = jnp.concatenate(
            [slabs[slab, mine, :].astype(BF16) for slab in range(depth)], axis=1
        )
        units = [index * merged + unit for unit in range(merged)]
        gate = dot(tokens, jnp.concatenate([gates[unit] for unit in units], axis=1))
        up = dot(tokens, jnp.concatenate([ups[unit] for unit in units], axis=1))
        activation = (gate / (1.0 + jnp.exp(-gate)) * up).astype(BF16)
        for first in range(0, depth, 4):
            lanes = slice(first * LANES, (first + 4) * LANES)
            made = dot(activation, jnp.concatenate([downs[unit, :, lanes] for unit in units], axis=0))
            for lane in range(4):
                slabs[first + lane, mine, :] = made[:, lane * LANES : (lane + 1) * LANES]

    core_far = lax.rem(core_peer, 2)
    row = head // 2

    def slab_rows(owner, place):
        return jnp.concatenate([slabs[owner * share + lane, place, :] for lane in range(share)], axis=1)

    def pair_copy(target, step):
        return remote(
            pair_out.at[target], pair_in.at[target], pair_send.at[step], pair_recv.at[step],
            (blk, core_peer),
        )

    def cross_copy(target, step):
        return remote(
            cross_out.at[target], cross_in.at[target], cross_send.at[step], cross_recv.at[step],
            (blk, side_peer),
        )

    def back_copy(step):
        target = lax.rem(blk + step, blocks)
        return remote(
            back_out.at[target], back_in.at[blk], back_send.at[step], back_recv.at[step],
            (target, head),
        )

    def back_arrival(step):
        source = lax.rem(blk - step + blocks, blocks)
        return remote(
            back_out.at[source], back_in.at[source], back_send.at[step], back_recv.at[step],
            (source, head),
        )

    def each(body):
        @pl.loop(1, blocks + 1)
        def _(count):
            step = lax.rem(count, blocks)
            target = lax.rem(blk + step, blocks)
            body(target, step, pl.ds(pl.multiple_of(target * room, 16), room))

    def to_core(target, step, place):
        for side in range(2):
            pair_out[target, side] = slab_rows(2 * side + core_far, place).astype(BF16)
        pair_copy(target, step).start()

    def to_side(target, step, place):
        pair_copy(target, step).wait_recv()
        other = slab_rows(side_peer, place) + pair_in[target, 1 - row].astype(F32)
        cross_out[target] = other.astype(BF16)
        cross_copy(target, step).start()

    def final(target, place):
        return (
            slab_rows(head, place) + pair_in[target, row].astype(F32) + cross_in[target].astype(F32)
        ).astype(BF16)

    each(to_core)
    each(to_side)

    @pl.loop(1, blocks)
    def _(step):
        target = lax.rem(blk + step, blocks)
        place = pl.ds(pl.multiple_of(target * room, 16), room)
        cross_copy(target, step).wait_recv()
        back_out[target] = final(target, place)
        back_copy(step).start()

    cross_copy(blk, 0).wait_recv()
    back_in[blk] = final(blk, pl.ds(pl.multiple_of(blk * room, 16), room))

    def weighted(source):
        return sum(
            lax.dot_general(
                combine[half, source], back_in[source], (((0,), (0,)), ((), ())),
                preferred_element_type=F32,
            )
            for half in range(2)
        )

    after[...] += weighted(blk)

    @pl.loop(1, blocks)
    def _(step):
        source = lax.rem(blk - step + blocks, blocks)
        back_arrival(step).wait_recv()
        after[...] += weighted(source)

    layer_out[...] = after[...].astype(BF16)

    for step in range(1, heads):
        share_copy(step).wait_send()

    @pl.loop(1, blocks)
    def _(step):
        all_copy(step).wait_send()
        back_copy(step).wait_send()

    @pl.loop(0, blocks)
    def _(step):
        source = lax.rem(blk - step + blocks, blocks)
        target = lax.rem(blk + step, blocks)
        core_copy(source, step).wait_send()
        side_copy(source, step).wait_send()
        relay_copy(source, step).wait_send()
        pair_copy(target, step).wait_send()
        cross_copy(target, step).wait_send()


def local(
    hidden, key_cache, value_cache, block_spans, cached_counts, expert_ids, gate_weights,
    attention_gain, mixture_gain, query_gain, key_gain,
    query_weight, key_weight, value_weight, output_weight,
    expert_gate, expert_up, expert_down,
):
    blocks, heads = lax.axis_size("blk"), lax.axis_size("head")
    block_index = lax.axis_index("blk")
    tokens, width = hidden.shape
    slots = key_cache.shape[0]
    local_width = key_cache.shape[1]

    whole_output = lax.all_gather(output_weight, "blk", axis=1, tiled=True)

    requests = jnp.arange(block_spans.shape[0])
    boundary = jnp.sum(
        jnp.where(requests[None, :] <= requests[:, None], block_spans[None, :], 0), axis=1
    )
    sources = block_index - jnp.arange(-REACH, REACH + 1, dtype=jnp.int32)
    request_of = lambda block: jnp.sum(
        (block[..., None] >= boundary).astype(jnp.int32), axis=-1
    )
    same = (
        (sources >= 0) & (sources < blocks) & (request_of(sources) == request_of(block_index))
    )
    live_count = jnp.sum(
        jnp.where(sources[:, None] == jnp.arange(blocks)[None, :], cached_counts[None, :], 0), axis=1
    )
    old_live = jnp.arange(slots, dtype=jnp.int32)[None, :] < live_count[:, None]
    mask = jnp.stack(
        [same[:, None] & old_live, jnp.broadcast_to(same[:, None], (same.shape[0], tokens))], axis=1
    ).astype(F32)[:, :, None, :]

    vmem = pl.BlockSpec(memory_space=pltpu.VMEM)
    hbm = pl.BlockSpec(memory_space=pl.ANY)
    dma = pltpu.SemaphoreType.DMA
    context = pl.pallas_call(
        functools.partial(attention_kernel, blocks, heads),
        out_shape=jax.ShapeDtypeStruct((tokens, local_width), BF16),
        in_specs=[vmem] * 10,
        out_specs=vmem,
        scratch_shapes=[
            pltpu.VMEM((heads, tokens, width), BF16),
            pltpu.VMEM((2 * REACH + 1, 4, slots, local_width), BF16),
            pltpu.VMEM((local_width // HD, tokens, HD), F32),
            pltpu.VMEM((local_width // HD, tokens, 1), F32),
            dma((heads,)), dma((heads,)),
            dma((2 * REACH + 1, 2)), dma((2 * REACH + 1, 2)),
        ],
        compiler_params=pltpu.CompilerParams(
            collective_id=0, has_side_effects=True, vmem_limit_bytes=24 << 20
        ),
        name="attention",
    )(
        hidden, key_cache, value_cache, attention_gain[None, :], query_gain[None, :],
        key_gain[None, :], mask, query_weight, key_weight, value_weight,
    )

    held = expert_gate.shape[0]
    merged = HP if held % HP == 0 else 1
    stride = held // merged
    room = -(-stride * CAP // 16) * 16
    named = jnp.sum(
        (expert_ids[:, :, None] == jnp.arange(EXPERTS, dtype=jnp.int32)).astype(F32), axis=1
    )
    earlier = jnp.arange(tokens)[:, None] > jnp.arange(tokens)[None, :]
    ranks = dot(earlier.astype(BF16), named.astype(BF16))
    rank = jnp.sum(
        jnp.where(expert_ids[:, :, None] == jnp.arange(EXPERTS, dtype=jnp.int32), ranks[:, None, :], 0.0),
        axis=2,
    ).astype(jnp.int32)
    matches = []
    scaled = []
    spots = jnp.arange(blocks * room, dtype=jnp.int32)
    for copy in range(HP // merged):
        if merged == HP:
            spot = expert_ids // stride * room + rank * stride + expert_ids % stride
        else:
            unit = expert_ids * HP + copy
            spot = unit // stride * room + rank * stride + unit % stride
        for choice in range(TOPK):
            matches.append(spots[:, None] == spot[:, choice][None, :])
            scaled.append(
                jnp.where(spots[:, None] == spot[:, choice][None, :], gate_weights[:, choice][None, :], 0.0)
            )
    dispatch = sum(match.astype(F32) for match in matches).astype(BF16)
    weights = sum(scaled)
    high = lax.reduce_precision(weights, 8, 7)
    combine = jnp.stack([high, weights - high]).astype(BF16)
    combine = combine.reshape(2, blocks, room, tokens)
    dispatch = dispatch.reshape(blocks, room, tokens)

    features = heads * width
    units = expert_gate.shape[2]
    row_block = (blocks, room, width)
    return pl.pallas_call(
        functools.partial(mixture_kernel, blocks, heads, stride, merged),
        out_shape=(
            jax.ShapeDtypeStruct((tokens, width), BF16),
            jax.ShapeDtypeStruct((tokens, width), BF16),
        ),
        in_specs=[vmem] * 6 + [hbm] * 3,
        out_specs=(vmem, vmem),
        scratch_shapes=[
            pltpu.VMEM((heads, tokens, width), BF16),
            pltpu.VMEM((heads, tokens, width), BF16),
            pltpu.VMEM((tokens, width), F32),
            pltpu.VMEM(row_block, BF16),
            pltpu.VMEM((heads,) + row_block, BF16),
            pltpu.VMEM((features // LANES, blocks * room, LANES), F32),
            pltpu.VMEM((held, features, units), BF16),
            pltpu.VMEM((held, features, units), BF16),
            pltpu.VMEM((held, units, features), BF16),
            pltpu.VMEM((blocks, 2, room, width), BF16),
            pltpu.VMEM((blocks, 2, room, width), BF16),
            pltpu.VMEM(row_block, BF16),
            pltpu.VMEM(row_block, BF16),
            pltpu.VMEM(row_block, BF16),
            pltpu.VMEM(row_block, BF16),
            dma((heads,)), dma((heads,)), dma((3, stride)),
        ]
        + [dma((blocks,))] * 14,
        compiler_params=pltpu.CompilerParams(
            collective_id=1, has_side_effects=True, vmem_limit_bytes=56 << 20
        ),
        name="mixture",
    )(
        context, whole_output, hidden, dispatch, combine, mixture_gain[None, :],
        expert_gate, expert_up, expert_down,
    )


def solution(mesh):
    placed = (
        P("blk", "head"),
        P("blk", "head"),
        P("blk", "head"),
        P(),
        P(),
        P("blk", None),
        P("blk", None),
        P(),
        P(),
        P(),
        P(),
        P(None, "head"),
        P(None, "head"),
        P(None, "head"),
        P("head", "blk"),
        P("blk", None, "head"),
        P("blk", None, "head"),
        P("blk", "head", None),
    )
    return jax.shard_map(
        local,
        mesh=mesh,
        in_specs=placed,
        out_specs=(P("blk", "head"), P("blk", "head")),
        check_vma=False,
    )
```

time: 440 us -> 142 us (0.32)
  waiting for transfers between devices: 172 us -> 0.68 us
  blocking collectives: 127 us -> 0 us
  Pallas kernels: 0 us -> 106 us
  local copies, waits for them, and re-layouts: 51.1 us -> 12.9 us
  starting transfers between devices: 29.6 us -> 0.04 us
  matrix products: 15.2 us -> 0.14 us
  other arithmetic: 20.4 us -> 7.08 us
  between operations: 22.7 us -> 14.1 us
    all_to_all x1 -> x0, blocking collectives: 119 us -> none  [send_whole(): lax.all_to_all(outgoing, 'blk', split_axis=0, concat_axis=0, tiled=True)]
    all_to_all x1 -> x0, waiting for transfers between devices: 111 us -> none  [local(): lax.all_to_all(produced.reshape(block_count, slots_here * CAP, produced.s...]
    pallas_call x0 -> x2, Pallas kernels: none -> 106 us  [the longest x1 68.7 us: local(): pl.pallas_call(functools.partial(mixture_kernel, blocks, heads, stride, m...]
    psum x1 -> x0, waiting for transfers between devices: 33 us -> none  [local(): lax.psum(attention.astype(jnp.bfloat16), 'head').astype(jnp.float32)]
    ppermute x6 -> x0, starting transfers between devices: 22.4 us -> none  [passed_along(): return lax.ppermute(block, axis, route)]
    reduce_scatter x1 -> x0, waiting for transfers between devices: 22 us -> none  [local(): lax.psum_scatter(mixture_partial.astype(jnp.bfloat16), 'head', scatter_di...]
    gather x2 -> x0, local copies, waits for them, and re-layouts: 18.3 us -> none  [the longest x1 12.1 us: local(): picked = flat_returned[slot_index.reshape(token_count, TOPK * HP)]]
    dot_general x9 -> x1, matrix products: 15.2 us -> 0.14 us  [dot(): return jnp.dot(left, right, preferred_element_type=F32)]
  transfers between devices with their start and end apart: 10 -> 1, of which waited for: 6 -> 0; matrix products, arithmetic and copies ran while one was open for 5% -> 6% of each run, Pallas kernels for 0% -> 27%
where the time goes in v1:
time: 142 us; the launch traced here: 141 us
  Pallas kernels  106 us (75%)
  between operations  14.1 us (10%)
  local copies, waits for them, and re-layouts  12.9 us (9%)
  other arithmetic  7.08 us (5%)
    pallas_call x1, Pallas kernels, local(): pl.pallas_call(functools.partial(mixture_kernel, blocks, heads, stride, m...  68.7 us
    pallas_call x1, Pallas kernels, local(): pl.pallas_call(functools.partial(attention_kernel, blocks, heads), out_sh...  37.4 us
    unnamed x22, local copies, waits for them, and re-layouts  12 us
  transfers between devices with their start and end apart: 1, of which 0 were waited for; matrix products, arithmetic and copies ran while one was open for 6% of the time, Pallas kernels for 27%

profile of v1, /device:TPU:10, one launch (start us, length us, event | category | flops | bytes accessed | tf_op | source)
XLA Modules:
  0.0 141.0 jit_solution(7477163592817049364)
XLA Ops:
  7.2 0.0 all-gather.2.cloned.1.call-start
  7.2 0.7 all-gather.2.cloned.1.call-update
  7.9 0.8 select_reduce_fusion.2
  8.7 0.6 fusion.10
  9.3 0.1 convert_reduce_fusion.1
  9.4 0.8 select_reduce_fusion.1
  10.2 0.7 compare_and_fusion
  10.9 0.1 fusion.4
  11.0 0.1 stack_broadcast_in_dim.2
  11.1 0.0 copy-start
  11.1 1.2 copy-done
  12.3 0.0 copy-start.1
  12.3 1.2 copy-done.1
  13.5 0.0 copy-start.2
  13.5 1.2 copy-done.2
  14.7 0.0 copy-start.3
  14.8 0.9 copy-done.3
  15.7 0.0 copy-start.5
  15.7 0.8 copy-done.5
  16.5 0.0 copy-start.6
  16.5 0.8 copy-done.6
  17.3 0.0 copy-start.7
  17.3 0.7 copy-done.7
  18.0 0.0 copy-start.8
  18.0 0.7 copy-done.8
  18.7 0.0 copy-start.9
  18.7 0.7 copy-done.9
  19.3 37.4 %attention.1.context = bf16[128,256]{1,0:T(8,128)(2,1)S(1)} custom-call(bf16[128,512]{1,0:T(8,128)(2,1)S(1)} %copy-done.3, bf16[128,256]{1,0:T(8,128)(2,1)S(1)} %copy-done.5, bf16[128,256]{1,0:T(8,128)(2,1)S(1)} %copy-done.6, f32[1,2048]{1,0:T(1,128)S(1)} %bitcast.25, f32[1,128]{1,0:T(1,128)S(1)} %bitcast.26, f32[1,128]{1,0:T(1,128)S(1)} %bitcast.27, ...), custom_call_target="tpu_custom_call" | custom-call | tf_op jit(solution)/shard_map/attention/pallas_call | solution.py:474
  56.7 0.0 copy-start.4
  56.7 0.6 copy-done.4
  57.4 0.7 convert_reduce_fusion
  58.1 0.1 fusion.1
  58.2 0.7 select_reduce_fusion
  58.9 0.7 fusion.7
  59.6 0.8 slice_bitcast_fusion.3
  60.5 0.2 reduce-precision_convert_fusion
  60.7 0.8 pad_maximum_fusion.combine
  61.5 0.9 add_convert_fusion.dispatch
  62.3 0.0 all-gather.2.cloned.1.call-done.output_weight
  62.3 68.7 %mixture.1 = (bf16[128,512]{1,0:T(8,128)(2,1)}, bf16[128,512]{1,0:T(8,128)(2,1)}) custom-call(bf16[128,256]{1,0:T(8,128)(2,1)} %copy-done.4, bf16[256,2048]{1,0:T(8,128)(2,1)} %all-gather.2.cloned.1.call-done.output_weight, bf16[128,512]{1,0:T(8,128)(2,1)} %hidden.3, bf16[8,80,128]{2,1,0:T(8,128)(2,1)} %add_convert_fusion.dispatch, ...), custom_call_target="tpu_custom_call" | custom-call | tf_op jit(solution)/shard_map/mixture/pallas_call | solution.py:533
  131.0 1.6 %copy.34 = bf16[128,512]{1,0:T(8,128)(2,1)} copy(bf16[128,512]{1,0:T(8,128)(2,1)} %get-tuple-element.14) | data formatting | bytes 262144
  132.6 1.6 %copy.35 = bf16[128,512]{1,0:T(8,128)(2,1)} copy(bf16[128,512]{1,0:T(8,128)(2,1)} %get-tuple-element.15) | data formatting | bytes 262144
  (5 shorter events, 0.0 us)
Async XLA Ops:
  7.2 55.2 %all-gather.2.cloned.1.call-start = ((), (), s32[]{:S(2)}) async-start(), calls=%async_computation | async-start | bytes 1179648 | tf_op jit(solution)/shard_map/all_gather | solution.py:450
  11.1 1.2 copy-start
  12.3 1.2 copy-start.1
  13.5 1.2 copy-start.2
  14.7 0.9 copy-start.3
  15.7 0.8 copy-start.5
  16.5 0.8 copy-start.6
  17.3 0.7 copy-start.7
  18.0 0.7 copy-start.8
  18.7 0.7 copy-start.9
  56.7 0.6 copy-start.4
Sparse Core Ops, SparseCore 0:
  10.0 45.4 all-gather.1

commit v2 on v1

--- a/solution.py
+++ b/solution.py
@@ -37,11 +37,20 @@
 def attention_kernel(
     blocks, heads,
     hidden, key_cache, value_cache, attention_gain, query_gain, key_gain, mask,
-    query_weight, key_weight, value_weight,
+    query_source, key_source, value_source,
     context,
+    query_weight, key_weight, value_weight, weight_sem,
     rows, pairs, numerator, denominator,
     row_send, row_recv, pair_send, pair_recv,
 ):
+    loads = [
+        pltpu.make_async_copy(source, target, weight_sem.at[kind])
+        for kind, (source, target) in enumerate(
+            ((key_source, key_weight), (value_source, value_weight), (query_source, query_weight))
+        )
+    ]
+    for load in loads:
+        load.start()
     blk, head = lax.axis_index("blk"), lax.axis_index("head")
     inside = lambda block: (block >= 0) & (block < blocks)
 
@@ -111,6 +120,8 @@
         ],
         axis=1,
     )
+    for load in loads:
+        load.wait()
     pairs[REACH, 2] = head_norm(dot(normed, key_weight[...]), key_gain[...])
     pairs[REACH, 3] = dot(normed, value_weight[...]).astype(BF16)
     send_pairs(1)
@@ -155,7 +166,7 @@
 
 def mixture_kernel(
     blocks, heads, stride, merged,
-    context, output_weight, hidden, dispatch, combine, mixture_gain,
+    context, output_weight, hidden, expert_ids, gate_weights, bases, mixture_gain,
     expert_gate, expert_up, expert_down,
     attention_out, layer_out,
     partial, arrived, after,
@@ -213,6 +224,33 @@
             (blk, target),
         )
 
+    tokens = hidden.shape[0]
+    experts = lax.broadcasted_iota(jnp.int32, (tokens, EXPERTS), 1)
+    chosen = [expert_ids[:, choice : choice + 1] == experts for choice in range(TOPK)]
+    named = sum(jnp.where(match, 1.0, 0.0) for match in chosen)
+    earlier = lax.broadcasted_iota(jnp.int32, (tokens, tokens), 0) > lax.broadcasted_iota(
+        jnp.int32, (tokens, tokens), 1
+    )
+    ranks = dot(jnp.where(earlier, 1.0, 0.0).astype(BF16), named.astype(BF16)) * stride
+    spots = [
+        (
+            jnp.sum(jnp.where(chosen[choice], ranks + bases[copy : copy + 1, :], 0.0), axis=1, keepdims=True),
+            gate_weights[:, choice : choice + 1],
+        )
+        for copy in range(HP // merged)
+        for choice in range(TOPK)
+    ]
+
+    def slot_row(block):
+        return (lax.broadcasted_iota(jnp.int32, (tokens, room), 1) + block * room).astype(F32)
+
+    def dispatched(block, values):
+        row = slot_row(block)
+        match = sum(jnp.where(spot == row, 1.0, 0.0) for spot, _ in spots).astype(BF16)
+        return lax.dot_general(
+            match, values, (((0,), (0,)), ((), ())), preferred_element_type=F32
+        ).astype(BF16)
+
     ctx = context[...]
     for index in range(heads):
         partial[index] = dot(ctx, output_weight[:, index * width : (index + 1) * width]).astype(BF16)
@@ -268,10 +306,10 @@
     @pl.loop(1, blocks)
     def _(step):
         target = lax.rem(blk + step, blocks)
-        outgoing[target] = dot(dispatch[target], rounded).astype(BF16)
+        outgoing[target] = dispatched(target, rounded)
         all_copy(step).start()
 
-    gathered[head, blk] = dot(dispatch[blk], rounded).astype(BF16)
+    gathered[head, blk] = dispatched(blk, rounded)
     core_copy(blk, 0).start()
     side_copy(blk, 0).start()
 
@@ -398,13 +436,11 @@
     back_in[blk] = final(blk, pl.ds(pl.multiple_of(blk * room, 16), room))
 
     def weighted(source):
-        return sum(
-            lax.dot_general(
-                combine[half, source], back_in[source], (((0,), (0,)), ((), ())),
-                preferred_element_type=F32,
-            )
-            for half in range(2)
-        )
+        row = slot_row(source)
+        weights = sum(jnp.where(spot == row, weight, 0.0) for spot, weight in spots)
+        high = weights.astype(BF16)
+        low = (weights - high.astype(F32)).astype(BF16)
+        return dot(high, back_in[source]) + dot(low, back_in[source])
 
     after[...] += weighted(blk)
 
@@ -474,9 +510,13 @@
     context = pl.pallas_call(
         functools.partial(attention_kernel, blocks, heads),
         out_shape=jax.ShapeDtypeStruct((tokens, local_width), BF16),
-        in_specs=[vmem] * 10,
+        in_specs=[vmem] * 7 + [hbm] * 3,
         out_specs=vmem,
         scratch_shapes=[
+            pltpu.VMEM(query_weight.shape, BF16),
+            pltpu.VMEM(key_weight.shape, BF16),
+            pltpu.VMEM(value_weight.shape, BF16),
+            dma((3,)),
             pltpu.VMEM((heads, tokens, width), BF16),
             pltpu.VMEM((2 * REACH + 1, 4, slots, local_width), BF16),
             pltpu.VMEM((local_width // HD, tokens, HD), F32),
@@ -485,7 +525,7 @@
             dma((2 * REACH + 1, 2)), dma((2 * REACH + 1, 2)),
         ],
         compiler_params=pltpu.CompilerParams(
-            collective_id=0, has_side_effects=True, vmem_limit_bytes=24 << 20
+            collective_id=0, has_side_effects=True, vmem_limit_bytes=56 << 20
         ),
         name="attention",
     )(
@@ -497,35 +537,8 @@
     merged = HP if held % HP == 0 else 1
     stride = held // merged
     room = -(-stride * CAP // 16) * 16
-    named = jnp.sum(
-        (expert_ids[:, :, None] == jnp.arange(EXPERTS, dtype=jnp.int32)).astype(F32), axis=1
-    )
-    earlier = jnp.arange(tokens)[:, None] > jnp.arange(tokens)[None, :]
-    ranks = dot(earlier.astype(BF16), named.astype(BF16))
-    rank = jnp.sum(
-        jnp.where(expert_ids[:, :, None] == jnp.arange(EXPERTS, dtype=jnp.int32), ranks[:, None, :], 0.0),
-        axis=2,
-    ).astype(jnp.int32)
-    matches = []
-    scaled = []
-    spots = jnp.arange(blocks * room, dtype=jnp.int32)
-    for copy in range(HP // merged):
-        if merged == HP:
-            spot = expert_ids // stride * room + rank * stride + expert_ids % stride
-        else:
-            unit = expert_ids * HP + copy
-            spot = unit // stride * room + rank * stride + unit % stride
-        for choice in range(TOPK):
-            matches.append(spots[:, None] == spot[:, choice][None, :])
-            scaled.append(
-                jnp.where(spots[:, None] == spot[:, choice][None, :], gate_weights[:, choice][None, :], 0.0)
-            )
-    dispatch = sum(match.astype(F32) for match in matches).astype(BF16)
-    weights = sum(scaled)
-    high = lax.reduce_precision(weights, 8, 7)
-    combine = jnp.stack([high, weights - high]).astype(BF16)
-    combine = combine.reshape(2, blocks, room, tokens)
-    dispatch = dispatch.reshape(blocks, room, tokens)
+    unit = jnp.arange(EXPERTS)[None, :] * (HP // merged) + jnp.arange(HP // merged)[:, None]
+    bases = (unit // stride * room + unit % stride).astype(F32)
 
     features = heads * width
     units = expert_gate.shape[2]
@@ -536,7 +549,7 @@
             jax.ShapeDtypeStruct((tokens, width), BF16),
             jax.ShapeDtypeStruct((tokens, width), BF16),
         ),
-        in_specs=[vmem] * 6 + [hbm] * 3,
+        in_specs=[vmem] * 7 + [hbm] * 3,
         out_specs=(vmem, vmem),
         scratch_shapes=[
             pltpu.VMEM((heads, tokens, width), BF16),
@@ -562,7 +575,7 @@
         ),
         name="mixture",
     )(
-        context, whole_output, hidden, dispatch, combine, mixture_gain[None, :],
+        context, whole_output, hidden, expert_ids, gate_weights, bases, mixture_gain[None, :],
         expert_gate, expert_up, expert_down,
     )
 

time: 142 us -> 140 us (0.986)
  waiting for transfers between devices: 0.68 us -> 16.6 us
  Pallas kernels: 106 us -> 98.5 us
  local copies, waits for them, and re-layouts: 12.9 us -> 6.04 us
  other arithmetic: 7.08 us -> 4.34 us
    all_gather x1, waiting for transfers between devices: 0.01 us -> 16 us  [local(): whole_output = lax.all_gather(output_weight, 'blk', axis=1, tiled=True)]
    unnamed x22 -> x4, local copies, waits for them, and re-layouts: 12 us -> 5.97 us
    pallas_call x1, Pallas kernels: 37.4 us -> 32.7 us  [local(): pl.pallas_call(functools.partial(attention_kernel, blocks, heads), out_sh...]
    pallas_call x1, Pallas kernels: 68.7 us -> 65.9 us  [local(): pl.pallas_call(functools.partial(mixture_kernel, blocks, heads, stride, m...]
    reduce_sum x2 -> x0, other arithmetic: 1.43 us -> none  [the longest x1 0.73 us: local(): jnp.sum(jnp.where(expert_ids[:, :, None] == jnp.arange(EXPERTS, dtype=jnp...]
  transfers between devices with their start and end apart: 1 -> 1, of which waited for: 0 -> 1; matrix products, arithmetic and copies ran while one was open for 6% -> 5% of each run, Pallas kernels for 27% -> 23%
where the time goes in v2:
time: 140 us
  Pallas kernels  98.5 us (70%)
  waiting for transfers between devices  16.6 us (12%)
  between operations  14.1 us (10%)
  local copies, waits for them, and re-layouts  6.04 us (4%)
  other arithmetic  4.34 us (3%)
    pallas_call x1, Pallas kernels, local(): pl.pallas_call(functools.partial(mixture_kernel, blocks, heads, stride, m...  65.9 us
    pallas_call x1, Pallas kernels, local(): pl.pallas_call(functools.partial(attention_kernel, blocks, heads), out_sh...  32.7 us
    all_gather x1, waiting for transfers between devices, local(): whole_output = lax.all_gather(output_weight, 'blk', axis=1, tiled=True)  16 us
    unnamed x4, local copies, waits for them, and re-layouts  5.97 us
  transfers between devices with their start and end apart: 1, of which 1 were waited for; matrix products, arithmetic and copies ran while one was open for 5% of the time, Pallas kernels for 23%

profile of v2, /device:TPU:10, one launch (start us, length us, event | category | flops | bytes accessed | tf_op | source)
XLA Modules:
  0.0 139.7 jit_solution(15213723665440375554)
XLA Ops:
  7.2 0.0 all-gather.2.cloned.1.call-start
  7.2 0.7 all-gather.2.cloned.1.call-update
  7.9 1.4 %copy.33.expert_ids = s32[128,4]{1,0:T(8,128)} copy(s32[128,4]{0,1:T(4,128)} %param.23) | data formatting | bytes 4096 | tf_op args[5]
  9.3 1.4 %copy.34.gate_weights = f32[128,4]{1,0:T(8,128)} copy(f32[128,4]{0,1:T(4,128)} %param.24) | data formatting | bytes 4096 | tf_op args[6]
  10.7 0.8 select_reduce_fusion.1
  11.5 0.7 fusion.5
  12.2 0.1 convert_reduce_fusion
  12.3 0.8 select_reduce_fusion
  13.1 0.7 compare_and_fusion
  13.9 0.1 fusion.1
  13.9 0.1 stack_broadcast_in_dim.2
  14.0 0.6 copy_convert_fusion
  14.6 32.7 %attention.1.context = bf16[128,256]{1,0:T(8,128)(2,1)} custom-call(bf16[128,512]{1,0:T(8,128)(2,1)} %hidden.3, bf16[128,256]{1,0:T(8,128)(2,1)} %key_cache.1, bf16[128,256]{1,0:T(8,128)(2,1)} %value_cache.1, f32[1,2048]{1,0:T(1,128)} %bitcast.8, f32[1,128]{1,0:T(1,128)} %bitcast.10, f32[1,128]{1,0:T(1,128)} %bitcast.11, f32[7,2,1,128]{3,2,1,0:T(1,128)} %bitcast.7, ...), custom_call_target="tpu_custom_call" | custom-call | tf_op jit(solution)/shard_map/attention/pallas_call | solution.py:510
  47.3 0.5 fusion.3.bases
  47.8 16.0 %all-gather.2.cloned.1.call-done.output_weight = bf16[256,2048]{1,0:T(8,128)(2,1)} async-done(((bf16[256,256]{1,0:T(8,128)(2,1)}), bf16[256,2048]{1,0:T(8,128)(2,1)}) %all-gather.2.cloned.1.call-update) | async-done | bytes 1048592 | tf_op jit(solution)/shard_map/all_gather | solution.py:486
  63.8 65.9 %mixture.1 = (bf16[128,512]{1,0:T(8,128)(2,1)}, bf16[128,512]{1,0:T(8,128)(2,1)}) custom-call(bf16[128,256]{1,0:T(8,128)(2,1)} %attention.1.context, bf16[256,2048]{1,0:T(8,128)(2,1)} %all-gather.2.cloned.1.call-done.output_weight, bf16[128,512]{1,0:T(8,128)(2,1)} %hidden.3, s32[128,4]{1,0:T(8,128)} %copy.33.expert_ids, f32[128,4]{1,0:T(8,128)} %copy.34.gate_weights, ...), custom_call_target="tpu_custom_call" | custom-call | tf_op jit(solution)/shard_map/mixture/pallas_call | solution.py:546
  129.7 1.6 %copy.38 = bf16[128,512]{1,0:T(8,128)(2,1)} copy(bf16[128,512]{1,0:T(8,128)(2,1)} %get-tuple-element.4) | data formatting | bytes 262144
  131.2 1.6 %copy.39 = bf16[128,512]{1,0:T(8,128)(2,1)} copy(bf16[128,512]{1,0:T(8,128)(2,1)} %get-tuple-element.5) | data formatting | bytes 262144
  (2 shorter events, 0.0 us)
Async XLA Ops:
  7.2 56.6 %all-gather.2.cloned.1.call-start = ((), (), s32[]{:S(2)}) async-start(), calls=%async_computation | async-start | bytes 1179648 | tf_op jit(solution)/shard_map/all_gather | solution.py:486
Sparse Core Ops, SparseCore 0:
  10.0 53.6 all-gather.1
